TPU v7x, 32 devices: a whole 2x2x4 slice. The times are simulated.
32 devices in a mesh: dp: 8 (over z, core), proto: 4 (over y, x).
Axes of the slice: x: 2, y: 2, z: 4, core: 2. Of those that a mesh axis runs over, the one named last changes fastest.
Arguments:
- teacher_feat: bfloat16 [1024, 256], P('dp'), may hold values from -8 to 8
- student_feat: bfloat16 [5120, 256], P('dp'), may hold values from -8 to 8
- teacher_weight: bfloat16 [256, 131072], P(None, 'proto'), may hold values from -0.375 to 0.375
- head_weight: bfloat16 [256, 131072], P(None, 'proto'), may hold values from -0.375 to 0.375
- pairing: int32 [5120], P('dp'), may hold values from 0 to 1023, as said below
Outputs:
- student_grad: float32 [5120, 256], P('dp', 'proto')
- head_grad: float32 [256, 131072], P('dp', 'proto')
Inputs may be any that keep to these rules, and one draw needn't show every extreme that they name: `pairing`: row r among the 640 student rows of one index j of dp is crop r // 64 of image m = r mod 64; it names teacher row j * 128 + m + 64 * v with view v of 0 or 1; crop 0 takes view 1 and crop 1 takes view 0.
All inputs are finite; a program needn't handle non-finite values.
Results may differ from a plain program's by a relative error of at most 0.0022.
Values sent between devices are 32-bit elements; how exact they have to be, the bound alone decides.
A program may use at most 320 MiB of HBM per device.

v0:
```python
import jax
import jax.numpy as jnp
from jax import lax
from jax.sharding import PartitionSpec as P

ITERS = 3


tiny_eps = 1e-06
teacher_temp = 0.04
student_temp = 0.1


def unit_rows(values):
    floats = values.astype(jnp.float32)
    inverse = lax.rsqrt(jnp.sum(floats * floats, axis=1, keepdims=True) + tiny_eps)
    return (floats * inverse, inverse)


def unit_columns(values):
    floats = values.astype(jnp.float32)
    inverse = lax.rsqrt(jnp.sum(floats * floats, axis=0, keepdims=True) + tiny_eps)
    return (floats * inverse, inverse)


def body(teacher_feat, student_feat, teacher_weight, head_weight, pairing):
    teach_rows = unit_rows(teacher_feat)[0].astype(jnp.bfloat16)
    teach_cols = unit_columns(teacher_weight)[0].astype(jnp.bfloat16)
    expo = jnp.exp(
        jnp.dot(teach_rows, teach_cols, preferred_element_type=jnp.float32) / teacher_temp
    )
    row_scale = jnp.ones((expo.shape[0],), jnp.float32)
    col_scale = jnp.ones((expo.shape[1],), jnp.float32)
    for iteration in range(ITERS):
        col_total = lax.psum(jnp.sum(expo * row_scale[:, None], axis=0), "dp")
        col_scale = 1.0 / col_total
        row_total = lax.psum(jnp.sum(expo * col_scale[None, :], axis=1), "proto")
        row_scale = 1.0 / row_total
    targets = expo * row_scale[:, None] * col_scale[None, :]
    stud_unit, stud_inverse = unit_rows(student_feat)
    stud_rows = stud_unit.astype(jnp.bfloat16)
    head_unit, head_inverse = unit_columns(head_weight)
    head_cols = head_unit.astype(jnp.bfloat16)
    logits = jnp.dot(stud_rows, head_cols, preferred_element_type=jnp.float32) / student_temp
    expo_s = jnp.exp(logits)
    totals = lax.psum(jnp.sum(expo_s, axis=1), "proto")
    local_pair = pairing - lax.axis_index("dp") * targets.shape[0]
    picked = jnp.take(targets, local_pair, axis=0)
    student_count = pairing.shape[0] * lax.axis_size("dp")
    grad_logits = ((expo_s / totals[:, None] - picked) / (student_temp * student_count)).astype(
        jnp.bfloat16
    )
    partial_value = lax.dot_general(
        grad_logits, head_cols, (((1,), (1,)), ((), ())), preferred_element_type=jnp.float32
    )
    width = stud_unit.shape[1]
    share = width // lax.axis_size("proto")
    offset = lax.axis_index("proto") * share
    own_part = lax.psum_scatter(partial_value, "proto", scatter_dimension=1, tiled=True)
    own_unit = lax.dynamic_slice_in_dim(stud_unit, offset, share, 1)
    along = lax.psum(jnp.sum(own_unit * own_part, axis=1), "proto")
    student_grad = (own_part - own_unit * along[:, None]) * stud_inverse
    dp_size = lax.axis_size("dp")
    row_count = width // dp_size
    head_part = lax.psum_scatter(
        lax.dot_general(
            stud_rows, grad_logits, (((0,), (0,)), ((), ())), preferred_element_type=jnp.float32
        ),
        "dp",
        scatter_dimension=0,
        tiled=True,
    )
    own_rows = lax.dynamic_slice_in_dim(head_unit, lax.axis_index("dp") * row_count, row_count, 0)
    inner = lax.psum(jnp.sum(own_rows * head_part, axis=0), "dp")
    head_grad = (head_part - own_rows * inner[None, :]) * head_inverse
    return (student_grad, head_grad)


def solution(mesh):
    return jax.shard_map(
        body,
        mesh=mesh,
        in_specs=(P("dp", None), P("dp", None), P(None, "proto"), P(None, "proto"), P("dp")),
        out_specs=(P("dp", "proto"), P("dp", "proto")),
        check_vma=False,
    )
```

profile of v0, /device:TPU:8, one launch (start us, length us, event | category | flops | bytes accessed | tf_op | source)
XLA Modules:
  0.0 858.9 jit_solution(8122889737575036984)
XLA Ops:
  7.2 0.0 copy-start.7
  7.2 0.0 all-reduce.6.cloned.1.call-start
  7.2 7.1 fusion.3
  14.4 0.0 copy-done.7
  14.4 0.1 fusion.15
  14.5 0.0 copy-start.6
  14.5 13.7 %fusion.19 = (f32[32768]{0:T(1024)}, f32[128,32768]{1,0:T(8,128)}) fusion(bf16[256,32768]{1,0:T(8,128)(2,1)} %param.7, f32[32768]{0:T(1024)S(1)} %add_rsqrt_fusion, bf16[128,256]{1,0:T(8,128)(2,1)S(1)} %copy-done.7, f32[128]{0:T(128)S(1)} %add_rsqrt_fusion.3), kind=kOutput, calls=%fused_computation.52 | convolution fusion | flops 2181103616 | bytes 33882624 | tf_op jit(solution)/shard_map/dot_general | solution.py:30
  28.2 0.0 all-reduce.6.cloned.1.call-update
  28.2 0.0 all-reduce.8.cloned.1.call-start
  28.2 0.0 copy-done.6
  28.2 0.2 copy.7
  28.5 0.0 copy-start
  28.5 0.1 fusion.11
  28.6 0.0 copy-start.4
  28.6 7.1 fusion.2
  35.7 0.0 copy-start.2
  35.7 36.0 %fusion = (f32[640]{0:T(1024)S(1)}, f32[640,32768]{1,0:T(8,128)}) fusion(f32[32768]{0:T(1024)S(1)} %add_rsqrt_fusion.1, bf16[256,32768]{1,0:T(8,128)(2,1)} %param.8, f32[640]{0:T(1024)S(1)} %add_rsqrt_fusion.2, bf16[640,256]{0,1:T(8,128)(2,1)S(1)} %copy.7), kind=kOutput, calls=%fused_computation.3 | convolution fusion | flops 10805017600 | bytes 101127168 | tf_op jit(solution)/shard_map/dot_general | solution.py:44
  71.7 0.0 copy-done
  71.7 0.0 copy-done.4
  71.7 0.0 copy-done.2
  71.7 11.1 %all-reduce.6.cloned.1.call-done = f32[32768]{0:T(1024)} async-done(((f32[32768]{0:T(1024)}), f32[32768]{0:T(1024)}) %all-reduce.6.cloned.1.call-update) | async-done | bytes 131088 | tf_op jit(solution)/shard_map/psum | solution.py:35
  82.8 0.9 broadcast_divide_fusion.2
  83.7 0.0 copy-start.9
  83.7 7.0 multiply_reduce_fusion.4
  90.7 9.8 %psum.65 = f32[128]{0:T(128)S(1)} all-reduce(f32[128]{0:T(128)S(1)} %multiply_reduce_fusion.4), channel_id=1, replica_groups=mesh['dp'=8,'proto'=4] {'proto'}, use_global_device_ids=true, to_apply=%region_9.0 | all-reduce | flops 128 | bytes 1024 | tf_op jit(solution)/shard_map/psum | solution.py:37
  100.6 7.9 multiply_reduce_fusion.3
  108.5 0.0 all-reduce.8.cloned.1.call-update
  108.5 0.2 all-reduce.10.cloned.1.call-start
  108.7 0.0 copy-done.9
  108.7 0.6 compare_and_fusion
  109.3 50.7 %all-reduce.8.cloned.1.call-done = f32[32768]{0:T(1024)} async-done(((f32[32768]{0:T(1024)}), f32[32768]{0:T(1024)}) %all-reduce.8.cloned.1.call-update) | async-done | bytes 131088 | tf_op jit(solution)/shard_map/psum | solution.py:35
  160.0 0.9 broadcast_divide_fusion.1
  161.0 7.0 multiply_reduce_fusion.2
  168.0 9.8 %psum.67 = f32[128]{0:T(128)S(1)} all-reduce(f32[128]{0:T(128)S(1)} %multiply_reduce_fusion.2), channel_id=1, replica_groups=mesh['dp'=8,'proto'=4] {'proto'}, use_global_device_ids=true, to_apply=%region_13.0 | all-reduce | flops 128 | bytes 1024 | tf_op jit(solution)/shard_map/psum | solution.py:37
  177.8 7.9 multiply_reduce_fusion.1
  185.7 0.0 all-reduce.10.cloned.1.call-update
  185.7 0.0 reduce-scatter.3.cloned.1.call-start
  185.8 51.5 %all-reduce.10.cloned.1.call-done = f32[32768]{0:T(1024)} async-done(((f32[32768]{0:T(1024)}), f32[32768]{0:T(1024)}) %all-reduce.10.cloned.1.call-update) | async-done | bytes 131088 | tf_op jit(solution)/shard_map/psum | solution.py:35
  237.3 0.9 broadcast_divide_fusion
  238.3 6.9 multiply_reduce_fusion
  245.2 10.6 %all-reduce = (f32[128]{0:T(128)S(1)}, f32[640]{0:T(1024)}) all-reduce(f32[128]{0:T(128)S(1)} %multiply_reduce_fusion, f32[640]{0:T(1024)S(1)} %get-tuple-element.8), channel_id=1, replica_groups=mesh['dp'=8,'proto'=4] {'proto'}, use_global_device_ids=true, to_apply=%region_17.0 | all-reduce | flops 768 | bytes 6144 | tf_op jit(solution)/shard_map/psum | solution.py:37
  255.8 11.6 %multiply_multiply_fusion = f32[128,32768]{1,0:T(8,128)} fusion(f32[128,32768]{1,0:T(8,128)} %get-tuple-element.7, f32[128]{0:T(128)S(1)} %broadcast_divide_fusion.3, f32[32768]{0:T(1024)S(1)} %broadcast_divide_fusion), kind=kLoop, calls=%fused_computation.13 | loop fusion | flops 8388608 | bytes 33686016 | tf_op jit(solution)/shard_map/mul | solution.py:39
  267.4 77.8 %gather_fusion = f32[640,32768]{1,0:T(8,128)} fusion(f32[128,32768]{1,0:T(8,128)} %multiply_multiply_fusion, s32[1024]{0:T(1024)S(1)} %pad_clamp_fusion), kind=kCustom, calls=%fused_computation | custom fusion | bytes 167774720 | tf_op jit(solution)/shard_map/jit(_take)/gather | solution.py:48
  345.2 0.0 copy-done.8
  345.2 0.0 copy-done.10
  345.2 65.5 %multiply_convert_fusion = bf16[640,32768]{1,0:T(8,128)(2,1)} fusion(f32[640,32768]{1,0:T(8,128)} %gather_fusion, f32[640,32768]{1,0:T(8,128)} %get-tuple-element.9, f32[640]{0:T(1024)S(1)} %copy-done.8, pred[640]{0:T(1024)(128)(4,1)S(1)} %copy-done.10), kind=kLoop, calls=%fused_computation.1 | loop fusion | flops 125829120 | bytes 209718400 | tf_op jit(solution)/shard_map/convert_element_type | solution.py:50
  410.7 0.0 copy-done.3
  410.7 0.0 copy-start.1
  410.7 0.0 copy-start.5
  410.7 23.6 %fusion.7 = f32[640,256]{0,1:T(8,128)} fusion(bf16[640,32768]{1,0:T(8,128)(2,1)} %multiply_convert_fusion, bf16[256,32768]{1,0:T(8,128)(2,1)} %param.8, f32[32768]{0:T(1024)S(1)} %copy-done.3), kind=kOutput, calls=%fused_computation.20 | convolution fusion | flops 10762584064 | bytes 59506688 | tf_op jit(solution)/shard_map/dot_general | solution.py:53
  434.3 0.0 reduce-scatter.3.cloned.1.call-update
  434.3 0.0 reduce-scatter.5.cloned.1.call-start
  434.4 31.2 %fusion.12 = f32[256,32768]{1,0:T(8,128)} fusion(bf16[640,32768]{1,0:T(8,128)(2,1)} %multiply_convert_fusion, bf16[640,256]{0,1:T(8,128)(2,1)S(1)} %copy-done.1, f32[640]{0:T(1024)S(1)} %copy-done.5), kind=kOutput, calls=%fused_computation.33 | convolution fusion | flops 10737909760 | bytes 75827712 | tf_op jit(solution)/shard_map/dot_general | solution.py:66
  465.6 0.0 reduce-scatter.5.cloned.1.call-update
  465.7 0.0 all-reduce.12.cloned.1.call-start
  465.8 18.9 %convert_multiply_fusion.2 = f32[256,32768]{1,0:T(8,128)} fusion(bf16[256,32768]{1,0:T(8,128)(2,1)} %param.8, f32[32768]{0:T(1024)S(1)} %copy-done.3), kind=kLoop, calls=%fused_computation.6 | loop fusion | flops 16777216 | bytes 50462720 | tf_op jit(solution)/shard_map/mul | solution.py:23
  484.6 0.9 multiply_reduce_fusion.6
  485.6 7.9 psum.70
  493.5 293.2 %reduce-scatter.5.cloned.1.call-done = f32[32,32768]{1,0:T(8,128)} async-done(((f32[256,32768]{1,0:T(8,128)}), f32[32,32768]{1,0:T(8,128)}) %reduce-scatter.5.cloned.1.call-update) | async-done | bytes 4194320 | tf_op jit(solution)/shard_map/reduce_scatter | solution.py:65
  786.7 4.7 multiply_reduce_fusion.5
  791.4 0.0 all-reduce.12.cloned.1.call-update
  791.4 1.6 subtract_multiply_fusion.1
  793.0 53.0 %all-reduce.12.cloned.1.call-done = f32[32768]{0:T(1024)} async-done(((f32[32768]{0:T(1024)}), f32[32768]{0:T(1024)}) %all-reduce.12.cloned.1.call-update) | async-done | bytes 131088 | tf_op jit(solution)/shard_map/psum | solution.py:74
  846.0 6.0 subtract_multiply_fusion
  (15 shorter events, 0.1 us)
Async XLA Ops:
  7.2 7.2 copy-start.7
  7.2 75.6 %all-reduce.6.cloned.1.call-start = ((), (), s32[]{:S(2)}) async-start(), calls=%async_computation.2 | async-start | bytes 262144 | tf_op jit(solution)/shard_map/psum | solution.py:35
  14.5 13.7 %copy-start.6 = (bf16[640,256]{1,0:T(8,128)(2,1)S(1)}, bf16[640,256]{1,0:T(8,128)(2,1)}, u32[]{:S(2)}) copy-start(bf16[640,256]{1,0:T(8,128)(2,1)} %param.6) | copy-start | bytes 983044
  28.2 131.9 %all-reduce.8.cloned.1.call-start = ((), (), s32[]{:S(2)}) async-start(), calls=%async_computation.3 | async-start | bytes 262144 | tf_op jit(solution)/shard_map/psum | solution.py:35
  28.5 43.2 %copy-start = (bf16[640,256]{0,1:T(8,128)(2,1)}, bf16[640,256]{0,1:T(8,128)(2,1)S(1)}, u32[]{:S(2)}) copy-start(bf16[640,256]{0,1:T(8,128)(2,1)S(1)} %copy.7) | copy-start | bytes 983044
  28.6 43.1 %copy-start.4 = (f32[640]{0:T(1024)}, f32[640]{0:T(1024)S(1)}, u32[]{:S(2)}) copy-start(f32[640]{0:T(1024)S(1)} %add_rsqrt_fusion.2) | copy-start | bytes 7684
  35.7 36.0 %copy-start.2 = (f32[32768]{0:T(1024)}, f32[32768]{0:T(1024)S(1)}, u32[]{:S(2)}) copy-start(f32[32768]{0:T(1024)S(1)} %add_rsqrt_fusion.1) | copy-start | bytes 393220
  83.7 25.0 %copy-start.9 = (s32[640]{0:T(1024)S(1)}, s32[640]{0:T(1024)}, u32[]{:S(2)}) copy-start(s32[640]{0:T(1024)} %param.9) | copy-start | bytes 7684
  108.5 128.8 %all-reduce.10.cloned.1.call-start = ((), (), s32[]{:S(2)}) async-start(), calls=%async_computation.4 | async-start | bytes 262144 | tf_op jit(solution)/shard_map/psum | solution.py:35
  185.7 298.9 %reduce-scatter.3.cloned.1.call-start = ((), (), s32[]{:S(2)}) async-start(), calls=%async_computation.5 | async-start | bytes 819200 | tf_op jit(solution)/shard_map/reduce_scatter | solution.py:59
  267.4 77.8 %copy-start.8 = (f32[640]{0:T(1024)S(1)}, f32[640]{0:T(1024)}, u32[]{:S(2)}) copy-start(f32[640]{0:T(1024)} %get-tuple-element.3) | copy-start | bytes 7684
  267.4 77.8 %copy-start.10 = (pred[640]{0:T(1024)(128)(4,1)S(1)}, pred[640]{0:T(1024)(128)(4,1)}, u32[]{:S(2)}) copy-start(pred[640]{0:T(1024)(128)(4,1)} %get-tuple-element.4) | copy-start | bytes 1924
  345.2 65.5 %copy-start.3 = (f32[32768]{0:T(1024)S(1)}, f32[32768]{0:T(1024)}, u32[]{:S(2)}) copy-start(f32[32768]{0:T(1024)} %copy-done.2) | copy-start | bytes 393220
  410.7 23.7 %copy-start.1 = (bf16[640,256]{0,1:T(8,128)(2,1)S(1)}, bf16[640,256]{0,1:T(8,128)(2,1)}, u32[]{:S(2)}) copy-start(bf16[640,256]{0,1:T(8,128)(2,1)} %copy-done) | copy-start | bytes 983044
  410.7 23.7 %copy-start.5 = (f32[640]{0:T(1024)S(1)}, f32[640]{0:T(1024)}, u32[]{:S(2)}) copy-start(f32[640]{0:T(1024)} %copy-done.4) | copy-start | bytes 7684
  434.3 352.3 %reduce-scatter.5.cloned.1.call-start = ((), (), s32[]{:S(2)}) async-start(), calls=%async_computation.6 | async-start | bytes 37748736 | tf_op jit(solution)/shard_map/reduce_scatter | solution.py:65
  465.7 380.4 %all-reduce.12.cloned.1.call-start = ((), (), s32[]{:S(2)}) async-start(), calls=%async_computation.7 | async-start | bytes 262144 | tf_op jit(solution)/shard_map/psum | solution.py:74
Sparse Core Ops, SparseCore 0:
  28.3 54.4 all-reduce.5
  108.6 51.3 all-reduce.7
  185.9 51.4 all-reduce.9
  434.5 23.5 reduce-scatter.2
  465.8 320.8 reduce-scatter.4
  791.5 54.4 all-reduce.11
where the time goes:
time: 862 us; the launch traced here: 859 us
  waiting for transfers between devices  460 us (53%)
  other arithmetic  164 us (19%)
  matrix products  104 us (12%)
  local copies, waits for them, and re-layouts  78.1 us (9%)
  blocking collectives  38.2 us (4%)
  between operations  14.3 us (2%)
    reduce_scatter x1, waiting for transfers between devices, body(): lax.psum_scatter(lax.dot_general(stud_rows, grad_logits, (((0,), (0,)), (...  293 us
    psum x3, waiting for transfers between devices, body(): col_total = lax.psum(jnp.sum(expo * row_scale[:, None], axis=0), 'dp')  113 us
    gather x1, local copies, waits for them, and re-layouts, body(): picked = jnp.take(targets, local_pair, axis=0)  77.8 us
    convert_element_type x1, other arithmetic, body(): ((expo_s / totals[:, None] - picked) / (student_temp * student_count)).as...  65.5 us
    psum x1, waiting for transfers between devices, body(): inner = lax.psum(jnp.sum(own_rows * head_part, axis=0), 'dp')  53 us
    dot_general x1, matrix products, body(): jnp.dot(stud_rows, head_cols, preferred_element_type=jnp.float32)  36 us
    dot_general x1, matrix products, body(): lax.dot_general(stud_rows, grad_logits, (((0,), (0,)), ((), ())), preferr...  31.2 us
    psum x3, blocking collectives, body(): row_total = lax.psum(jnp.sum(expo * col_scale[None, :], axis=1), 'proto')  30.3 us
  transfers between devices with their start and end apart: 6, of which 5 were waited for; matrix products, arithmetic and copies ran while one was open for 11% of the time, Pallas kernels for 0%

commit v1 on v0

v1 whole, which is shorter than its diff:
```python
import jax
import jax.numpy as jnp
from jax import lax
from jax.sharding import PartitionSpec as P

ITERS = 3


tiny_eps = 1e-06
teacher_temp = 0.04
student_temp = 0.1
BOTH = ("dp", "proto")


def unit_rows(values):
    floats = values.astype(jnp.float32)
    inverse = lax.rsqrt(jnp.sum(floats * floats, axis=1, keepdims=True) + tiny_eps)
    return (floats * inverse, inverse)


def unit_columns(values):
    floats = values.astype(jnp.float32)
    inverse = lax.rsqrt(jnp.sum(floats * floats, axis=0, keepdims=True) + tiny_eps)
    return (floats * inverse, inverse)


def dot(a, b, da, db):
    return lax.dot_general(a, b, (((da,), (db,)), ((), ())), preferred_element_type=jnp.float32)


def split_sum(values):
    high = values.astype(jnp.bfloat16)
    return high, (values - high.astype(jnp.float32)).astype(jnp.bfloat16)


def body(teacher_feat, student_feat, teacher_weight, head_weight, pairing):
    dp, me = lax.axis_size("dp"), lax.axis_index("dp")
    protos = lax.axis_size("proto")
    teach, width = teacher_feat.shape
    stud = student_feat.shape[0]
    images = teach // 2
    crops = stud // images
    mine = head_weight.shape[1] // dp
    scale = 1.0 / (student_temp * stud * dp)

    teach_unit = unit_rows(teacher_feat)[0]
    stud_unit, stud_inverse = unit_rows(student_feat)
    view = (pairing - me * teach) // images
    kept = stud_unit.astype(jnp.bfloat16).astype(jnp.float32).reshape(crops, images, width)
    second = (view == 1).reshape(crops, images, 1)
    pair_sums = jnp.concatenate(
        [jnp.sum(jnp.where(second, 0.0, kept), 0), jnp.sum(jnp.where(second, kept, 0.0), 0)], 0
    )
    packet = jnp.concatenate([stud_unit, teach_unit, pair_sums], 0)
    packet = lax.optimization_barrier(lax.all_gather(packet, "dp", axis=0, tiled=False))
    stud_rows = packet[:, :stud].reshape(dp * stud, width).astype(jnp.bfloat16)
    teach_rows = packet[:, stud : stud + teach].reshape(dp * teach, width).astype(jnp.bfloat16)
    sums = packet[:, stud + teach :].reshape(dp * teach, width)

    teach_cols = unit_columns(lax.dynamic_slice_in_dim(teacher_weight, me * mine, mine, 1))[0].astype(jnp.bfloat16)
    head_unit, head_inverse = unit_columns(lax.dynamic_slice_in_dim(head_weight, me * mine, mine, 1))
    head_cols = head_unit.astype(jnp.bfloat16)

    expo = jnp.exp(dot(teach_rows, teach_cols, 1, 0) / teacher_temp)
    expo_s = jnp.exp(dot(stud_rows, head_cols, 1, 0) / student_temp)
    totals = lax.psum(jnp.sum(expo_s, axis=1), BOTH)
    expo_s = expo_s.astype(jnp.bfloat16)
    raw = dot(expo_s, head_cols, 1, 1)

    row_scale = jnp.ones((expo.shape[0],), jnp.float32)
    for iteration in range(ITERS):
        col_scale = 1.0 / jnp.sum(expo * row_scale[:, None], axis=0)
        row_scale = 1.0 / lax.psum(jnp.sum(expo * col_scale[None, :], axis=1), BOTH)
    targets = (expo * row_scale[:, None] * col_scale[None, :]).astype(jnp.bfloat16)

    aim = dot(targets, head_cols, 1, 1)
    block = jnp.concatenate(
        [(raw / totals[:, None]).reshape(dp, stud, width), aim.reshape(dp, teach, width)], 1
    )
    block = lax.psum_scatter(block, "dp", scatter_dimension=0, tiled=False)
    block = lax.psum_scatter(block, "proto", scatter_dimension=1, tiled=True)
    share = width // protos
    offset = lax.axis_index("proto") * share
    aims = block[stud:].reshape(2, 1, images, share)
    picked = jnp.where(second, aims[1], aims[0]).reshape(stud, share)
    own_part = (block[:stud] - picked) * scale
    own_unit = lax.dynamic_slice_in_dim(stud_unit, offset, share, 1)
    along = lax.psum(jnp.sum(own_unit * own_part, axis=1), "proto")
    student_grad = (own_part - own_unit * along[:, None]) * stud_inverse

    scaled = (stud_rows.astype(jnp.float32) / totals[:, None]).astype(jnp.bfloat16)
    high, low = split_sum(sums)
    weight_grad = (dot(scaled, expo_s, 0, 0) - dot(high, targets, 0, 0) - dot(low, targets, 0, 0)) * scale
    inner = jnp.sum(head_unit * weight_grad, axis=0, keepdims=True)
    head_grad = (weight_grad - head_unit * inner) * head_inverse
    head_grad = lax.all_to_all(head_grad, "dp", split_axis=0, concat_axis=1, tiled=True)
    return (student_grad, head_grad)


def solution(mesh):
    return jax.shard_map(
        body,
        mesh=mesh,
        in_specs=(P("dp", None), P("dp", None), P(None, "proto"), P(None, "proto"), P("dp")),
        out_specs=(P("dp", "proto"), P("dp", "proto")),
        check_vma=False,
    )
```

time: 862 us -> 527 us (0.61)
  waiting for transfers between devices: 460 us -> 162 us
  other arithmetic: 164 us -> 69.2 us
  blocking collectives: 38.2 us -> 132 us
  local copies, waits for them, and re-layouts: 78.1 us -> 13.2 us
  matrix products: 104 us -> 126 us
    reduce_scatter x2 -> x1, waiting for transfers between devices: 293 us -> 11 us  [body(): block = lax.psum_scatter(block, 'dp', scatter_dimension=0, tiled=False)]
    psum x4 -> x0, waiting for transfers between devices: 166 us -> none  [the longest x3 113 us: body(): col_total = lax.psum(jnp.sum(expo * row_scale[:, None], axis=0), 'dp')]
    psum x3, blocking collectives: 30.3 us -> 122 us  [body(): row_scale = 1.0 / lax.psum(jnp.sum(expo * col_scale[None, :], axis=1), BOTH)]
    all_to_all x0 -> x1, waiting for transfers between devices: none -> 81.7 us  [body(): lax.all_to_all(head_grad, 'dp', split_axis=0, concat_axis=1, tiled=True)]
    gather x1 -> x0, local copies, waits for them, and re-layouts: 77.8 us -> none  [body(): picked = jnp.take(targets, local_pair, axis=0)]
    all_gather x0 -> x1, waiting for transfers between devices: none -> 68.9 us  [body(): lax.all_gather(packet, 'dp', axis=0, tiled=False)]
    convert_element_type x1 -> x3, other arithmetic: 65.5 us -> 9.7 us  [the longest x1 7.09 us: body(): (expo * row_scale[:, None] * col_scale[None, :]).astype(jnp.bfloat16)]
    mul x3 -> x1, other arithmetic: 36.5 us -> 5.78 us  [body(): head_grad = (weight_grad - head_unit * inner) * head_inverse]
  transfers between devices with their start and end apart: 6 -> 4, of which waited for: 5 -> 3; matrix products, arithmetic and copies ran while one was open for 11% -> 12% of each run, Pallas kernels for 0% -> 0%
where the time goes in v1:
time: 527 us; the launch traced here: 521 us
  waiting for transfers between devices  162 us (31%)
  blocking collectives  132 us (25%)
  matrix products  126 us (24%)
  other arithmetic  69.2 us (13%)
  between operations  14 us (3%)
  local copies, waits for them, and re-layouts  13.2 us (3%)
    dot_general x7, matrix products, dot(): lax.dot_general(a, b, (((da,), (db,)), ((), ())), preferred_element_type=...  126 us
    psum x3, blocking collectives, body(): row_scale = 1.0 / lax.psum(jnp.sum(expo * col_scale[None, :], axis=1), BOTH)  122 us
    all_to_all x1, waiting for transfers between devices, body(): lax.all_to_all(head_grad, 'dp', split_axis=0, concat_axis=1, tiled=True)  81.7 us
    all_gather x1, waiting for transfers between devices, body(): lax.all_gather(packet, 'dp', axis=0, tiled=False)  68.9 us
    reduce_sum x3, other arithmetic, body(): row_scale = 1.0 / lax.psum(jnp.sum(expo * col_scale[None, :], axis=1), BOTH)  21.1 us
    reduce_sum x2, other arithmetic, body(): col_scale = 1.0 / jnp.sum(expo * row_scale[:, None], axis=0)  14.3 us
    reduce_scatter x1, waiting for transfers between devices, body(): block = lax.psum_scatter(block, 'dp', scatter_dimension=0, tiled=False)  11 us
  transfers between devices with their start and end apart: 4, of which 3 were waited for; matrix products, arithmetic and copies ran while one was open for 12% of the time, Pallas kernels for 0%

profile of v1, /device:TPU:8, one launch (start us, length us, event | category | flops | bytes accessed | tf_op | source)
XLA Modules:
  0.0 521.2 jit_solution(3710696260960163318)
XLA Ops:
  7.2 0.0 all-gather.3.cloned.1.call-start
  7.2 0.9 fusion.45
  8.2 0.7 fusion.47
  8.9 0.1 broadcast_in_dim.65
  9.0 1.2 fusion.40
  10.1 0.0 copy-start.3
  10.2 0.9 convert_multiply_fusion.6
  11.1 1.1 fusion.55
  12.2 0.0 copy-start.1
  12.2 0.2 fusion.41
  12.4 0.0 copy-done.3
  12.4 0.6 copy-done.1
  13.1 1.0 pad_maximum_fusion.1
  14.0 0.0 all-gather.3.cloned.1.call-update
  14.1 0.0 reduce-scatter.5.cloned.1.call-start
  14.1 3.1 fusion.24
  17.3 68.9 %all-gather.3.cloned.1.call-done = f32[7168,256]{1,0:T(8,128)} async-done(((f32[896,256]{1,0:T(8,128)}), f32[7168,256]{1,0:T(8,128)}) %all-gather.3.cloned.1.call-update) | async-done | bytes 7340048 | tf_op jit(solution)/shard_map/all_gather | solution.py:55
  86.2 2.3 slice.36
  88.5 0.0 copy-done.5
  88.5 3.5 convert.5
  92.0 0.2 slice.31
  92.2 9.2 %fusion.57 = (f32[4096]{0:T(1024)S(1)}, f32[1024,4096]{1,0:T(8,128)}) fusion(bf16[1024,256]{1,0:T(8,128)(2,1)S(1)} %bitcast.53, f32[4096]{0:T(1024)S(1)} %add_rsqrt_fusion, bf16[256,32768]{1,0:T(8,128)(2,1)} %param.7, s32[]{:T(128)S(6)} %select_n.28), kind=kOutput, calls=%fused_computation.84 | convolution fusion | flops 2159013888 | bytes 19431428 | tf_op jit(solution)/shard_map/dot_general | solution.py:28
  101.4 7.1 %multiply_reduce_fusion.4 = f32[1024]{0:T(1024)S(1)} fusion(f32[1024,4096]{1,0:T(8,128)} %get-tuple-element.17, f32[4096]{0:T(1024)S(1)} %broadcast_divide_fusion.2), kind=kLoop, calls=%fused_computation.8 | loop fusion | flops 8387584 | bytes 16797696 | tf_op jit(solution)/shard_map/reduce_sum | solution.py:73
  108.5 41.8 %psum.36 = f32[1024]{0:T(1024)S(1)} all-reduce(f32[1024]{0:T(1024)S(1)} %multiply_reduce_fusion.4), channel_id=1, replica_groups=mesh['dp'=8,'proto'=4] {'dp','proto'}, use_global_device_ids=true, to_apply=%region_10.11 | all-reduce | flops 1024 | bytes 8192 | tf_op jit(solution)/shard_map/psum | solution.py:73
  150.3 7.2 %multiply_reduce_fusion.3 = f32[4096]{0:T(1024)S(1)} fusion(f32[1024,4096]{1,0:T(8,128)} %get-tuple-element.17, f32[1024]{0:T(1024)S(1)} %broadcast_divide_fusion.5), kind=kLoop, calls=%fused_computation.7 | loop fusion | flops 8384512 | bytes 16797696 | tf_op jit(solution)/shard_map/reduce_sum | solution.py:72
  157.5 7.1 %multiply_reduce_fusion.2 = f32[1024]{0:T(1024)S(1)} fusion(f32[1024,4096]{1,0:T(8,128)} %get-tuple-element.17, f32[4096]{0:T(1024)S(1)} %broadcast_divide_fusion.1), kind=kLoop, calls=%fused_computation.6 | loop fusion | flops 8387584 | bytes 16797696 | tf_op jit(solution)/shard_map/reduce_sum | solution.py:73
  164.6 38.9 %psum.37 = f32[1024]{0:T(1024)S(1)} all-reduce(f32[1024]{0:T(1024)S(1)} %multiply_reduce_fusion.2), channel_id=1, replica_groups=mesh['dp'=8,'proto'=4] {'dp','proto'}, use_global_device_ids=true, to_apply=%region_13.14 | all-reduce | flops 1024 | bytes 8192 | tf_op jit(solution)/shard_map/psum | solution.py:73
  203.5 7.2 %multiply_reduce_fusion.1 = f32[4096]{0:T(1024)S(1)} fusion(f32[1024,4096]{1,0:T(8,128)} %get-tuple-element.17, f32[1024]{0:T(1024)S(1)} %broadcast_divide_fusion.4), kind=kLoop, calls=%fused_computation.5 | loop fusion | flops 8384512 | bytes 16797696 | tf_op jit(solution)/shard_map/reduce_sum | solution.py:72
  210.7 6.9 %multiply_reduce_fusion = f32[1024]{0:T(1024)S(1)} fusion(f32[1024,4096]{1,0:T(8,128)} %get-tuple-element.17, f32[4096]{0:T(1024)S(1)} %broadcast_divide_fusion), kind=kLoop, calls=%fused_computation.4 | loop fusion | flops 8387584 | bytes 16797696 | tf_op jit(solution)/shard_map/reduce_sum | solution.py:73
  217.6 31.1 %fusion = (f32[5120]{0:T(1024)S(1)}, f32[5120,4096]{0,1:T(8,128)}) fusion(bf16[5120,256]{1,0:T(8,128)(2,1)S(1)} %bitcast.46, f32[4096]{0:T(1024)S(1)} %add_rsqrt_fusion.1, bf16[256,32768]{1,0:T(8,128)(2,1)} %param.8, s32[]{:T(128)S(6)} %select_n.28), kind=kOutput, calls=%fused_computation.1 | convolution fusion | flops 10782501888 | bytes 88641536 | tf_op jit(solution)/shard_map/dot_general | solution.py:28
  248.7 41.7 %all-reduce = (f32[1024]{0:T(1024)S(1)}, f32[5120]{0:T(1024)S(1)}) all-reduce(f32[1024]{0:T(1024)S(1)} %multiply_reduce_fusion, f32[5120]{0:T(1024)S(1)} %get-tuple-element.18), channel_id=1, replica_groups=mesh['dp'=8,'proto'=4] {'dp','proto'}, use_global_device_ids=true, to_apply=%region_16.17 | all-reduce | flops 6144 | bytes 49152 | tf_op jit(solution)/shard_map/psum | solution.py:73
  290.4 7.1 %multiply_convert_fusion = bf16[1024,4096]{1,0:T(8,128)(2,1)S(1)} fusion(f32[1024,4096]{1,0:T(8,128)} %get-tuple-element.17, f32[1024]{0:T(1024)S(1)} %broadcast_divide_fusion.3, f32[4096]{0:T(1024)S(1)} %broadcast_divide_fusion), kind=kLoop, calls=%fused_computation.3 | loop fusion | flops 12582912 | bytes 25186304 | tf_op jit(solution)/shard_map/convert_element_type | solution.py:74
  297.5 0.0 copy-start
  297.5 6.5 %fusion.31 = f32[1024,256]{1,0:T(8,128)} fusion(bf16[1024,4096]{1,0:T(8,128)(2,1)S(1)} %multiply_convert_fusion, f32[4096]{0:T(1024)S(1)} %add_rsqrt_fusion.1, bf16[256,32768]{1,0:T(8,128)(2,1)} %param.8, s32[]{:T(128)S(6)} %select_n.28), kind=kOutput, calls=%fused_computation.34 | convolution fusion | flops 2150629376 | bytes 11550724 | tf_op jit(solution)/shard_map/dot_general | solution.py:28
  304.0 0.0 copy-done
  304.0 31.7 %fusion.6 = f32[5120,256]{1,0:T(8,128)} fusion(f32[5120,4096]{0,1:T(8,128)} %get-tuple-element.19, f32[5120]{0:T(1024)S(1)} %get-tuple-element.9, f32[4096]{0:T(1024)S(1)} %add_rsqrt_fusion.1, bf16[256,32768]{1,0:T(8,128)(2,1)} %param.8, s32[]{:T(128)S(6)} %select_n.28), kind=kOutput, calls=%fused_computation.13 | convolution fusion | flops 10783817728 | bytes 91262976 | tf_op jit(solution)/shard_map/dot_general | solution.py:28
  335.7 6.0 %pad_maximum_fusion = f32[8,768,256]{2,1,0:T(8,128)} fusion(f32[8,128,256]{2,1,0:T(8,128)} %bitcast.55, f32[8,640,256]{2,1,0:T(8,128)} %bitcast.50), kind=kLoop, calls=%fused_computation.12 | loop fusion | flops 1572864 | bytes 12582912 | tf_op jit(solution)/shard_map/concatenate | solution.py:77
  341.7 0.0 reduce-scatter.5.cloned.1.call-update
  341.7 0.0 slice-start
  341.7 1.5 fusion.36
  343.2 0.0 slice-start.1
  343.2 7.9 %fusion.59 = f32[256,4096]{1,0:T(8,128)} fusion(bf16[1024,256]{1,0:T(8,128)(2,1)S(1)} %get-tuple-element.10, bf16[1024,4096]{1,0:T(8,128)(2,1)} %copy-done), kind=kOutput, calls=%fused_computation.86 | convolution fusion | flops 2147483648 | bytes 13107200 | tf_op jit(solution)/shard_map/dot_general | solution.py:28
  351.2 0.0 slice-done
  351.2 0.0 slice-done.1
  351.2 4.5 fusion.58
  355.7 35.1 %fusion.21 = (f32[4096]{0:T(1024)S(1)}, f32[256,4096]{1,0:T(8,128)}) fusion(f32[4096]{0:T(1024)S(1)} %add_rsqrt_fusion.1, bf16[256,32768]{1,0:T(8,128)(2,1)} %param.8, s32[]{:T(128)S(6)} %select_n.28, f32[256,4096]{1,0:T(8,128)} %fusion.59, f32[256,4096]{1,0:T(8,128)} %fusion.58, f32[5120,4096]{0,1:T(8,128)} %get-tuple-element.19, ...), kind=kOutput, calls=%fused_computation.25 | convolution fusion | flops 10790629376 | bytes 101240832 | tf_op jit(solution)/shard_map/dot_general | solution.py:28
  390.8 5.8 %fusion.23 = f32[256,4096]{1,0:T(8,128)} fusion(f32[256,4096]{1,0:T(8,128)} %get-tuple-element.21, f32[4096]{0:T(1024)S(1)} %get-tuple-element.20, f32[4096]{0:T(1024)S(1)} %add_rsqrt_fusion.1, bf16[256,32768]{1,0:T(8,128)(2,1)} %param.8, s32[]{:T(128)S(6)} %select_n.28), kind=kLoop, calls=%fused_computation.27 | loop fusion | flops 5242880 | bytes 10518532 | tf_op jit(solution)/shard_map/mul | solution.py:95
  396.6 4.7 all-to-all-start
  401.3 0.0 reduce-scatter.7.cloned.1.call-start
  401.3 11.0 %reduce-scatter.5.cloned.1.call-done = f32[1,768,256]{2,1,0:T(8,128)} async-done(((f32[8,768,256]{2,1,0:T(8,128)}), f32[1,768,256]{2,1,0:T(8,128)}) %reduce-scatter.5.cloned.1.call-update) | async-done | bytes 786448 | tf_op jit(solution)/shard_map/reduce_scatter | solution.py:80
  412.2 2.3 copy.17
  414.5 0.0 reduce-scatter.7.cloned.1.call-update
  414.5 0.0 copy-start.4
  414.6 81.7 %all-to-all-done = f32[8,32,4096]{2,1,0:T(8,128)} async-done(((f32[8,32,4096]{2,1,0:T(8,128)}), f32[8,32,4096]{2,1,0:T(8,128)}, u32[]{:S(2)}, u32[]{:S(2)}) %all-to-all-start) | async-done | bytes 4194336 | tf_op jit(solution)/shard_map/all_to_all | solution.py:96
  496.3 4.7 copy.22
  501.0 0.9 fusion.56
  501.9 0.9 slice.33
  502.8 0.1 copy.20
  502.9 0.1 copy.21
  503.0 0.2 copy.19
  503.2 0.4 multiply_reduce_fusion.5
  503.5 9.9 %psum.39 = f32[640]{0:T(1024)S(1)} all-reduce(f32[640]{0:T(1024)S(1)} %multiply_reduce_fusion.5), channel_id=1, replica_groups=mesh['dp'=8,'proto'=4] {'proto'}, use_global_device_ids=true, to_apply=%region_20.21 | all-reduce | flops 640 | bytes 5120 | tf_op jit(solution)/shard_map/psum | solution.py:88
  513.4 0.4 subtract_multiply_fusion
  513.8 0.8 copy.16
  (19 shorter events, 0.1 us)
Async XLA Ops:
  7.2 79.0 %all-gather.3.cloned.1.call-start = ((), (), s32[]{:S(2)}) async-start(), calls=%async_computation.4 | async-start | bytes 8257536 | tf_op jit(solution)/shard_map/all_gather | solution.py:55
  8.9 79.6 %copy-start.5 = (pred[640]{0:T(1024)(128)(4,1)}, pred[640]{0:T(1024)(128)(4,1)S(1)}, u32[]{:S(2)}) copy-start(pred[640]{0:T(1024)(128)(4,1)S(1)} %fusion.47) | copy-start | bytes 1924
  10.1 2.3 copy-start.3
  12.2 0.9 copy-start.1
  14.1 398.2 %reduce-scatter.5.cloned.1.call-start = ((), (), s32[]{:S(2)}) async-start(), calls=%async_computation.3 | async-start | bytes 7077888 | tf_op jit(solution)/shard_map/reduce_scatter | solution.py:80
  297.5 6.5 %copy-start = (bf16[1024,4096]{1,0:T(8,128)(2,1)}, bf16[1024,4096]{1,0:T(8,128)(2,1)S(1)}, u32[]{:S(2)}) copy-start(bf16[1024,4096]{1,0:T(8,128)(2,1)S(1)} %multiply_convert_fusion) | copy-start | bytes 25165828
  341.7 9.5 %slice-start = ((s8[8388608]{0:T(1024)(128)(4,1)}), s8[4194304]{0:T(1024)(128)(4,1)S(1)}, s32[]{:S(2)}) async-start(s8[8388608]{0:T(1024)(128)(4,1)} %bitcast.43), calls=%async_computation.6 | async-start | bytes 8388608
  343.2 7.9 %slice-start.1 = ((s8[8388608]{0:T(1024)(128)(4,1)}), s8[4194304]{0:T(1024)(128)(4,1)S(1)}, s32[]{:S(2)}) async-start(s8[8388608]{0:T(1024)(128)(4,1)} %bitcast.43), calls=%async_computation.7 | async-start | bytes 8388608
  396.6 99.7 %all-to-all-start = ((f32[8,32,4096]{2,1,0:T(8,128)}), f32[8,32,4096]{2,1,0:T(8,128)}, u32[]{:S(2)}, u32[]{:S(2)}) async-start(f32[8,32,4096]{2,1,0:T(8,128)} %bitcast.45), calls=%async_computation.1 | async-start | bytes 8388608 | tf_op jit(solution)/shard_map/all_to_all | solution.py:96
  401.3 99.7 %reduce-scatter.7.cloned.1.call-start = ((), (), s32[]{:S(2)}) async-start(), calls=%async_computation.5 | async-start | bytes 983040
  414.5 88.6 %copy-start.2 = (f32[640,256]{1,0:T(8,128)S(1)}, f32[640,256]{1,0:T(8,128)}, u32[]{:S(2)}) copy-start(f32[640,256]{1,0:T(8,128)} %copy-done.1) | copy-start | bytes 1966084
  414.5 88.7 %copy-start.6 = (pred[640]{0:T(1024)(128)(4,1)S(1)}, pred[640]{0:T(1024)(128)(4,1)}, u32[]{:S(2)}) copy-start(pred[640]{0:T(1024)(128)(4,1)} %copy-done.5) | copy-start | bytes 1924
  414.5 98.9 %copy-start.4 = (f32[640]{0:T(1024)S(1)}, f32[640]{0:T(1024)}, u32[]{:S(2)}) copy-start(f32[640]{0:T(1024)} %copy-done.3) | copy-start | bytes 7684
Sparse Core Ops, SparseCore 0:
  14.2 71.9 all-gather.2
  341.8 70.3 reduce-scatter.4
  415.1 41.5 reduce-scatter.6
